TPU v7x, 32 devices: a whole 2x2x4 slice. The times are simulated.
32 devices in a mesh: row: 4 (over x, core), col: 4 (over z), depth: 2 (over y).
Axes of the slice: x: 2, y: 2, z: 4, core: 2. Of those that a mesh axis runs over, the one named last changes fastest.
Arguments:
- left_blocks: float32 [512, 64, 64], P(('row', 'col', 'depth')), may hold values from -6 to 6
- right_blocks: float32 [512, 64, 64], P(('row', 'col', 'depth')), may hold values from -0.25 to 0.25
- triples: int32 [3, 16384], P(None, ('row', 'col', 'depth')), may hold values from 0 to 128, as said below
Outputs:
- product_blocks: float32 [2048, 64, 64], P(('row', 'col', 'depth'))
Inputs may be any that keep to these rules, and one draw needn't show every extreme that they name: With G = 4 contraction groups per panel and layer, left slot number i * G + g is the block of block row i and group g, and right slot j * G + g the block of group g and block column j. Each device keeps 128 distinct (block row, block column) pairs, and out slot o names the o-th of them. A used triple takes the left block (i, g) and the right block (g, j) of one group g and sends their product to the kept slot of (i, j); a device's used triples are distinct and come first among its 512. An unused triple is (0, 0, 128). Every device has at least 128 used triples, and some device has all 512 used.
All inputs are finite; a program needn't handle non-finite values.
Results may differ from a plain program's by a relative error of at most 0.0003.
Values sent between devices are 32-bit elements; how exact they have to be, the bound alone decides.
A program may use at most 128 MiB of HBM per device.

v0:
```python
import math

import jax
import jax.numpy as jnp
from jax import lax
from jax.sharding import PartitionSpec as P

PC = 128


def per_device(left_blocks, right_blocks, triples):
    order = left_blocks.shape[1]
    left_panel = lax.all_gather(left_blocks, "col", axis=0, tiled=True)
    right_panel = lax.all_gather(right_blocks, "row", axis=0, tiled=True)
    slot_count = triples.shape[1]
    group_size = math.gcd(slot_count, 128)
    left_slots = triples[0]
    right_slots = triples[1]
    out_slots = triples[2]

    def accumulate(step_index, partial_value):
        start = step_index * group_size
        left_pick = lax.dynamic_slice_in_dim(left_slots, start, group_size)
        right_pick = lax.dynamic_slice_in_dim(right_slots, start, group_size)
        out_pick = lax.dynamic_slice_in_dim(out_slots, start, group_size)
        products = jnp.einsum(
            "tij,tjk->tik",
            left_panel[left_pick],
            right_panel[right_pick],
            precision=lax.Precision.HIGHEST,
            preferred_element_type=jnp.float32,
        )
        return partial_value.at[out_pick].add(products)

    partial_value = jnp.zeros((PC + 1, order, order), jnp.float32)
    partial_value = lax.fori_loop(0, slot_count // group_size, accumulate, partial_value)
    partial_value = partial_value[:PC]
    layers = lax.axis_size("depth")
    share = PC // layers
    summed = lax.psum(partial_value, "depth")
    kept = lax.dynamic_slice_in_dim(summed, lax.axis_index("depth") * share, share, 0)
    return kept


def solution(mesh):
    placed = (
        P(("row", "col", "depth"), None, None),
        P(("row", "col", "depth"), None, None),
        P(None, ("row", "col", "depth")),
    )
    return jax.shard_map(
        per_device,
        mesh=mesh,
        in_specs=placed,
        out_specs=P(("row", "col", "depth"), None, None),
        check_vma=False,
    )
```

profile of v0, /device:TPU:0, one launch (start us, length us, event | category | flops | bytes accessed | tf_op | source)
XLA Modules:
  0.0 356.4 jit_solution(10122739365268403232)
XLA Ops:
  6.5 0.0 all-gather.3.cloned.1.call-start
  6.5 0.7 all-gather.3.cloned.1.call-update
  7.3 0.0 all-gather.5.cloned.1.call-start
  7.3 0.7 all-gather.5.cloned.1.call-update
  8.0 0.0 all-reduce.2.cloned.1.call-start
  8.1 0.8 fusion
  8.9 48.7 %all-gather.3.cloned.1.call-done = f32[64,64,64]{2,1,0:T(8,128)} async-done(((f32[16,64,64]{2,1,0:T(8,128)}), f32[64,64,64]{2,1,0:T(8,128)}) %all-gather.3.cloned.1.call-update) | async-done | bytes 1048592 | tf_op jit(solution)/shard_map/all_gather | solution.py:13
  57.6 0.0 copy-start
  57.6 22.9 %all-gather.5.cloned.1.call-done = f32[64,64,64]{2,1,0:T(8,128)} async-done(((f32[16,64,64]{2,1,0:T(8,128)}), f32[64,64,64]{2,1,0:T(8,128)}) %all-gather.5.cloned.1.call-update) | async-done | bytes 1048592 | tf_op jit(solution)/shard_map/all_gather | solution.py:14
  80.5 2.5 broadcast_in_dim.24
  83.0 0.0 copy-done
  83.0 149.1 %while.13 = (s32[]{:T(128)}, f32[129,64,64]{2,1,0:T(8,128)}, s32[512]{0:T(512)S(1)}, s32[512]{0:T(512)S(1)}, f32[64,64,64]{2,1,0:T(8,128)S(1)}, /*index=5*/s32[5...) while((s32[]{:T(128)}, f32[129,64,64]{2,1,0:T(8,128)}, ...), condition=%wide.region_2.0_spmd, body=%wide.region_0.0_spmd.sunk | while | flops 403180672 | bytes 20985508 | solution.py:36
  83.0 0.1 compare_select_fusion.6
  83.1 2.8 gather_fusion
  85.9 4.3 %gather_fusion.1 = f32[128,64,64]{2,1,0:T(8,128)} fusion(f32[64,64,64]{2,1,0:T(8,128)} %get-tuple-element.224, s32[1024]{0:T(1024)S(1)} %pad_clamp_fusion.5), kind=kCustom, calls=%fused_computation.1.clone.1 | custom fusion | bytes 4194816 | tf_op jit(solution)/shard_map/while/body/eval_jaxpr/gather | solution.py:29
  90.2 9.8 %fusion.9 = f32[128,64,64]{2,1,0:T(8,128)} fusion(f32[128,64,64]{2,1,0:T(8,128)} %gather_fusion, f32[128,64,64]{2,1,0:T(8,128)} %gather_fusion.1), kind=kOutput, calls=%fused_computation.10.clone.1 | convolution fusion | flops 402653184 | bytes 6291456 | tf_op jit(solution)/shard_map/while/body/eval_jaxpr/tij,tjk->tik/dot_general | solution.py:26
  100.0 0.1 compare_select_fusion.5
  100.1 20.2 %scatter_fusion = f32[129,64,64]{2,1,0:T(8,128)} fusion(f32[129,64,64]{2,1,0:T(8,128)} %get-tuple-element.208, s32[128]{0:T(128)S(1)} %compare_select_fusion.5, f32[128,64,64]{2,1,0:T(8,128)} %fusion.9), kind=kCustom, calls=%fused_computation.2.clone.1 | custom fusion | flops 524288 | bytes 6291968 | tf_op jit(solution)/shard_map/while/body/eval_jaxpr/scatter-add | solution.py:33
  120.3 0.1 compare_select_fusion.6
  120.3 2.8 gather_fusion
  123.1 4.3 %gather_fusion.1 = f32[128,64,64]{2,1,0:T(8,128)} fusion(f32[64,64,64]{2,1,0:T(8,128)} %get-tuple-element.224, s32[1024]{0:T(1024)S(1)} %pad_clamp_fusion.5), kind=kCustom, calls=%fused_computation.1.clone.1 | custom fusion | bytes 4194816 | tf_op jit(solution)/shard_map/while/body/eval_jaxpr/gather | solution.py:29
  127.5 9.8 %fusion.9 = f32[128,64,64]{2,1,0:T(8,128)} fusion(f32[128,64,64]{2,1,0:T(8,128)} %gather_fusion, f32[128,64,64]{2,1,0:T(8,128)} %gather_fusion.1), kind=kOutput, calls=%fused_computation.10.clone.1 | convolution fusion | flops 402653184 | bytes 6291456 | tf_op jit(solution)/shard_map/while/body/eval_jaxpr/tij,tjk->tik/dot_general | solution.py:26
  137.3 0.1 compare_select_fusion.5
  137.4 20.2 %scatter_fusion = f32[129,64,64]{2,1,0:T(8,128)} fusion(f32[129,64,64]{2,1,0:T(8,128)} %get-tuple-element.208, s32[128]{0:T(128)S(1)} %compare_select_fusion.5, f32[128,64,64]{2,1,0:T(8,128)} %fusion.9), kind=kCustom, calls=%fused_computation.2.clone.1 | custom fusion | flops 524288 | bytes 6291968 | tf_op jit(solution)/shard_map/while/body/eval_jaxpr/scatter-add | solution.py:33
  157.6 0.1 compare_select_fusion.6
  157.6 2.8 gather_fusion
  160.4 4.3 %gather_fusion.1 = f32[128,64,64]{2,1,0:T(8,128)} fusion(f32[64,64,64]{2,1,0:T(8,128)} %get-tuple-element.224, s32[1024]{0:T(1024)S(1)} %pad_clamp_fusion.5), kind=kCustom, calls=%fused_computation.1.clone.1 | custom fusion | bytes 4194816 | tf_op jit(solution)/shard_map/while/body/eval_jaxpr/gather | solution.py:29
  164.8 9.8 %fusion.9 = f32[128,64,64]{2,1,0:T(8,128)} fusion(f32[128,64,64]{2,1,0:T(8,128)} %gather_fusion, f32[128,64,64]{2,1,0:T(8,128)} %gather_fusion.1), kind=kOutput, calls=%fused_computation.10.clone.1 | convolution fusion | flops 402653184 | bytes 6291456 | tf_op jit(solution)/shard_map/while/body/eval_jaxpr/tij,tjk->tik/dot_general | solution.py:26
  174.6 0.1 compare_select_fusion.5
  174.7 20.1 %scatter_fusion = f32[129,64,64]{2,1,0:T(8,128)} fusion(f32[129,64,64]{2,1,0:T(8,128)} %get-tuple-element.208, s32[128]{0:T(128)S(1)} %compare_select_fusion.5, f32[128,64,64]{2,1,0:T(8,128)} %fusion.9), kind=kCustom, calls=%fused_computation.2.clone.1 | custom fusion | flops 524288 | bytes 6291968 | tf_op jit(solution)/shard_map/while/body/eval_jaxpr/scatter-add | solution.py:33
  194.8 0.1 compare_select_fusion.6
  194.9 2.8 gather_fusion
  197.7 4.3 %gather_fusion.1 = f32[128,64,64]{2,1,0:T(8,128)} fusion(f32[64,64,64]{2,1,0:T(8,128)} %get-tuple-element.224, s32[1024]{0:T(1024)S(1)} %pad_clamp_fusion.5), kind=kCustom, calls=%fused_computation.1.clone.1 | custom fusion | bytes 4194816 | tf_op jit(solution)/shard_map/while/body/eval_jaxpr/gather | solution.py:29
  202.0 9.8 %fusion.9 = f32[128,64,64]{2,1,0:T(8,128)} fusion(f32[128,64,64]{2,1,0:T(8,128)} %gather_fusion, f32[128,64,64]{2,1,0:T(8,128)} %gather_fusion.1), kind=kOutput, calls=%fused_computation.10.clone.1 | convolution fusion | flops 402653184 | bytes 6291456 | tf_op jit(solution)/shard_map/while/body/eval_jaxpr/tij,tjk->tik/dot_general | solution.py:26
  211.8 0.1 compare_select_fusion.5
  211.9 20.1 %scatter_fusion = f32[129,64,64]{2,1,0:T(8,128)} fusion(f32[129,64,64]{2,1,0:T(8,128)} %get-tuple-element.208, s32[128]{0:T(128)S(1)} %compare_select_fusion.5, f32[128,64,64]{2,1,0:T(8,128)} %fusion.9), kind=kCustom, calls=%fused_computation.2.clone.1 | custom fusion | flops 524288 | bytes 6291968 | tf_op jit(solution)/shard_map/while/body/eval_jaxpr/scatter-add | solution.py:33
  232.0 4.7 %slice.15 = f32[128,64,64]{2,1,0:T(8,128)} slice(f32[129,64,64]{2,1,0:T(8,128)} %get-tuple-element.129), slice={[0:128], [0:64], [0:64]} | slice | bytes 4194304 | tf_op jit(solution)/shard_map/slice | solution.py:37
  236.8 0.0 all-reduce.2.cloned.1.call-update
  236.8 109.9 %all-reduce.2.cloned.1.call-done = f32[128,64,64]{2,1,0:T(8,128)} async-done(((f32[128,64,64]{2,1,0:T(8,128)}), f32[128,64,64]{2,1,0:T(8,128)}) %all-reduce.2.cloned.1.call-update) | async-done | bytes 2097168 | tf_op jit(solution)/shard_map/psum | solution.py:40
  346.7 3.2 constant_dynamic-slice_fusion
  (8 shorter events, 0.1 us)
Async XLA Ops:
  6.5 51.1 %all-gather.3.cloned.1.call-start = ((), (), s32[]{:S(2)}) async-start(), calls=%async_computation | async-start | bytes 2621440 | tf_op jit(solution)/shard_map/all_gather | solution.py:13
  7.3 73.2 %all-gather.5.cloned.1.call-start = ((), (), s32[]{:S(2)}) async-start(), calls=%async_computation.1 | async-start | bytes 2621440 | tf_op jit(solution)/shard_map/all_gather | solution.py:14
  8.0 338.7 %all-reduce.2.cloned.1.call-start = ((), (), s32[]{:S(2)}) async-start(), calls=%async_computation.2 | async-start | bytes 8388608 | tf_op jit(solution)/shard_map/psum | solution.py:40
  57.6 25.4 %copy-start = (f32[64,64,64]{2,1,0:T(8,128)S(1)}, f32[64,64,64]{2,1,0:T(8,128)}, u32[]{:S(2)}) copy-start(f32[64,64,64]{2,1,0:T(8,128)} %all-gather.3.cloned.1.call-done) | copy-start | bytes 3145732
Sparse Core Ops, SparseCore 0:
  8.9 48.6 all-gather.2
  59.2 21.2 all-gather.4
  236.9 109.7 all-reduce.1
where the time goes:
time: 358 us; the launch traced here: 356 us
  waiting for transfers between devices  183 us (51%)
  other arithmetic  81.2 us (23%)
  local copies, waits for them, and re-layouts  39.7 us (11%)
  matrix products  39.3 us (11%)
  between operations  13.1 us (4%)
    psum x1, waiting for transfers between devices, per_device(): summed = lax.psum(partial_value, 'depth')  110 us
    scatter-add x4, other arithmetic, accumulate(): return partial_value.at[out_pick].add(products)  80.6 us
    all_gather x1, waiting for transfers between devices, per_device(): left_panel = lax.all_gather(left_blocks, 'col', axis=0, tiled=True)  48.7 us
    dot_general x4, matrix products, accumulate(): jnp.einsum('tij,tjk->tik', left_panel[left_pick], right_panel[right_pick]...  39.3 us
    all_gather x1, waiting for transfers between devices, per_device(): right_panel = lax.all_gather(right_blocks, 'row', axis=0, tiled=True)  22.9 us
    gather x4, local copies, waits for them, and re-layouts, accumulate(): right_panel[right_pick]  17.3 us
    gather x4, local copies, waits for them, and re-layouts, accumulate(): left_panel[left_pick]  11.2 us
  transfers between devices with their start and end apart: 3, of which 3 were waited for; matrix products, arithmetic and copies ran while one was open for 0% of the time, Pallas kernels for 0%

commit v1 on v0

v1 whole, which is shorter than its diff:
```python
import functools

import jax
import jax.numpy as jnp
from jax import lax
from jax.experimental import pallas as pl
from jax.experimental.pallas import tpu as pltpu
from jax.sharding import PartitionSpec as P

PC = 128
LANES = 128
CHUNK_ROWS = 16
UNROLL_PAIRS = 8
MESH = pl.DeviceIdType.MESH


def split_bf16(value):
    high = value.astype(jnp.bfloat16)
    low = (value - high.astype(jnp.float32)).astype(jnp.bfloat16)
    return high, low


def kernel(
    sizes,
    left_ref,
    right_ref,
    triples_ref,
    out_ref,
    left_all,
    right_all,
    right_split,
    left_split,
    mask_ref,
    mask_rows,
    code_rows,
    codes,
    part_send,
    part_recv,
    part_own,
    left_send_sem,
    left_recv_sem,
    right_send_sem,
    right_recv_sem,
    core_send_sem,
    core_recv_sem,
    part_send_sem,
    part_recv_sem,
    code_sem,
):
    n_row, n_col, n_depth, order, groups, local_rows, share, chunks = sizes
    row = lax.axis_index("row")
    col = lax.axis_index("col")
    depth = lax.axis_index("depth")
    outers = n_row // 2
    core = row % 2
    outer = row // 2
    other_core = outer * 2 + (1 - core)
    width = groups * order
    pairs = share // 2

    def turn(index, step, count):
        return lax.rem(index + step, count)

    barrier = pltpu.get_barrier_semaphore()
    greeted = 0
    for step in range(1, n_col):
        pl.semaphore_signal(barrier, inc=1, device_id={"col": turn(col, step, n_col)}, device_id_type=MESH)
        greeted += 1
    for step in range(1, outers):
        pl.semaphore_signal(
            barrier, inc=1, device_id={"row": turn(outer, step, outers) * 2 + core}, device_id_type=MESH
        )
        greeted += 1
    pl.semaphore_signal(barrier, inc=1, device_id={"row": other_core}, device_id_type=MESH)
    greeted += 1
    for step in range(1, n_depth):
        pl.semaphore_signal(barrier, inc=1, device_id={"depth": turn(depth, step, n_depth)}, device_id_type=MESH)
        greeted += 1

    for i in range(local_rows):
        for g in range(0, groups, 2):
            pair = jnp.concatenate([left_ref[i * groups + g], left_ref[i * groups + g + 1]], axis=-1)
            for q in range(chunks):
                left_all[q, col, i, :, g * order : (g + 2) * order] = pair[q * CHUNK_ROWS : (q + 1) * CHUNK_ROWS]
    for j in range(0, local_rows, 2):
        for g in range(groups):
            pair = jnp.concatenate([right_ref[j * groups + g], right_ref[(j + 1) * groups + g]], axis=-1)
            right_all[row, j // 2, g * order : (g + 1) * order, :] = pair

    pl.semaphore_wait(barrier, greeted)

    def left_copy(q, step):
        return pltpu.make_async_remote_copy(
            src_ref=left_all.at[q, col],
            dst_ref=left_all.at[q, col],
            send_sem=left_send_sem.at[q, step - 1],
            recv_sem=left_recv_sem.at[q, step - 1],
            device_id={"col": turn(col, step, n_col)},
            device_id_type=MESH,
        )

    def right_copy(step):
        return pltpu.make_async_remote_copy(
            src_ref=right_all.at[row],
            dst_ref=right_all.at[row],
            send_sem=right_send_sem.at[step - 1],
            recv_sem=right_recv_sem.at[step - 1],
            device_id={"row": turn(outer, step, outers) * 2 + core},
            device_id_type=MESH,
        )

    def core_copy(step):
        source = turn(outer + outers, -step, outers) * 2 + core
        return pltpu.make_async_remote_copy(
            src_ref=right_all.at[source],
            dst_ref=right_all.at[source],
            send_sem=core_send_sem.at[step],
            recv_sem=core_recv_sem.at[step],
            device_id={"row": other_core},
            device_id_type=MESH,
        )

    def part_copy(q, step):
        return pltpu.make_async_remote_copy(
            src_ref=part_send.at[q, step - 1],
            dst_ref=part_recv.at[q, step - 1],
            send_sem=part_send_sem.at[q, step - 1],
            recv_sem=part_recv_sem.at[q, step - 1],
            device_id={"depth": turn(depth, step, n_depth)},
            device_id_type=MESH,
        )

    for step in range(1, outers):
        right_copy(step).start()
    for step in range(n_col - 1, 0, -1):
        left_copy(0, step).start()
    core_copy(0).start()
    for q in range(1, chunks):
        for step in range(n_col - 1, 0, -1):
            left_copy(q, step).start()

    left_slot = triples_ref[0:1, :]
    right_slot = triples_ref[1:2, :]
    out_slot = triples_ref[2:3, :]
    group_of = lax.rem(left_slot, groups)
    code = lax.div(left_slot, groups) * 1024 + lax.div(right_slot, groups)
    lane = lax.broadcasted_iota(jnp.int32, (16, width), 1)
    for k in range(0, PC, 16):
        here = out_slot == lax.broadcasted_iota(jnp.int32, (16, out_slot.shape[1]), 0) + k
        found = jnp.max(jnp.where(here, code, 0), axis=1, keepdims=True)
        code_rows[k : k + 16, :] = jnp.broadcast_to(found, (16, LANES))
        used = jnp.zeros((16, width), jnp.float32)
        for g in range(groups):
            at_group = jnp.max(
                jnp.where(here & (group_of == g), 1.0, 0.0).astype(jnp.float32), axis=1, keepdims=True
            )
            used = jnp.where(lane // order == g, at_group, used)
        mask_rows[k : k + 16, :] = used
    code_copy = pltpu.make_async_copy(code_rows, codes, code_sem)
    code_copy.start()

    def spread(k, carry):
        mask_ref[k] = jnp.broadcast_to(mask_rows[pl.ds(k, 1), :], (CHUNK_ROWS, width)).astype(jnp.bfloat16)
        return carry

    lax.fori_loop(0, PC, spread, 0, unroll=8)
    code_copy.wait()

    lower = lax.broadcasted_iota(jnp.int32, (order, LANES), 1) < order

    def split_right(shard):
        for j in range(local_rows // 2):
            for g in range(groups):
                rows = slice(g * order, (g + 1) * order)
                value = right_all[shard, j, rows, :]
                high = value.astype(jnp.bfloat16).astype(jnp.float32)
                low = pltpu.roll(value - high, order, 1)
                at = shard * local_rows + 2 * j
                right_split[at, rows, :] = jnp.where(lower, high, low).astype(jnp.bfloat16)
                right_split[at + 1, rows, :] = jnp.where(lower, low, high).astype(jnp.bfloat16)

    split_right(row)
    core_copy(0).wait_recv()
    split_right(other_core)
    for step in range(1, outers):
        right_copy(step).wait_recv()
        core_copy(step).start()
        split_right(turn(outer + outers, -step, outers) * 2 + core)
    for step in range(1, outers):
        core_copy(step).wait_recv()
        split_right(turn(outer + outers, -step, outers) * 2 + (1 - core))

    lane_low = lax.broadcasted_iota(jnp.int32, (CHUNK_ROWS, LANES), 1) < order

    def one_slot(q, k):
        found = codes[k, 0]
        picked = left_split[q, found // 1024]
        used = mask_ref[k]
        picked = picked * jnp.concatenate([used, used], axis=0)
        both = jnp.dot(picked, right_split[found % 1024], preferred_element_type=jnp.float32)
        both = both[:CHUNK_ROWS] + both[CHUNK_ROWS:]
        return both + pltpu.roll(both, order, 1)

    def products(q, first, target):
        def body(turn_index, carry):
            for inner in range(UNROLL_PAIRS):
                p = turn_index * UNROLL_PAIRS + inner
                k = first + 2 * p
                target[p] = jnp.where(lane_low, one_slot(q, k), one_slot(q, k + 1))
            return carry

        lax.fori_loop(0, pairs // UNROLL_PAIRS, body, 0)

    def finish(q):
        for step in range(1, n_depth):
            part_copy(q, step).wait_recv()

        def body(p, carry):
            total = part_own[q, p]
            for step in range(1, n_depth):
                total = total + part_recv[q, step - 1, p]
            rows = pl.ds(q * CHUNK_ROWS, CHUNK_ROWS)
            out_ref[2 * p, rows, :] = total[:, :order]
            out_ref[2 * p + 1, rows, :] = pltpu.roll(total, order, 1)[:, :order]
            return carry

        lax.fori_loop(0, pairs, body, 0, unroll=min(8, pairs))

    for q in range(chunks):
        for step in range(1, n_col):
            left_copy(q, step).wait_recv()
        for shard in range(n_col):
            for i in range(local_rows):
                high, low = split_bf16(left_all[q, shard, i])
                left_split[q, shard * local_rows + i, :CHUNK_ROWS, :] = high
                left_split[q, shard * local_rows + i, CHUNK_ROWS:, :] = low
        for step in range(1, n_depth):
            partner = turn(depth, step, n_depth)
            products(q, partner * share, part_send.at[q, step - 1])
            part_copy(q, step).start()
        products(q, depth * share, part_own.at[q])
        if q > 0:
            finish(q - 1)
    finish(chunks - 1)

    for q in range(chunks):
        for step in range(1, n_col):
            left_copy(q, step).wait_send()
        for step in range(1, n_depth):
            part_copy(q, step).wait_send()
    for step in range(1, outers):
        right_copy(step).wait_send()
    for step in range(outers):
        core_copy(step).wait_send()


def per_device(sizes, left_blocks, right_blocks, triples):
    n_row, n_col, n_depth, order, groups, local_rows, share, chunks = sizes
    width = groups * order
    pairs = share // 2
    f32, bf16, i32 = jnp.float32, jnp.bfloat16, jnp.int32
    dma = pltpu.SemaphoreType.DMA
    return pl.pallas_call(
        functools.partial(kernel, sizes),
        out_shape=jax.ShapeDtypeStruct((share, order, order), f32),
        in_specs=[pl.BlockSpec(memory_space=pltpu.VMEM)] * 3,
        out_specs=pl.BlockSpec(memory_space=pltpu.VMEM),
        scratch_shapes=[
            pltpu.VMEM((chunks, n_col, local_rows, CHUNK_ROWS, width), f32),
            pltpu.VMEM((n_row, local_rows // 2, width, LANES), f32),
            pltpu.VMEM((n_row * local_rows, width, LANES), bf16),
            pltpu.VMEM((chunks, n_col * local_rows, 2 * CHUNK_ROWS, width), bf16),
            pltpu.VMEM((PC, CHUNK_ROWS, width), bf16),
            pltpu.VMEM((PC, width), f32),
            pltpu.VMEM((PC, LANES), i32),
            pltpu.SMEM((PC, LANES), i32),
            pltpu.VMEM((chunks, n_depth - 1, pairs, CHUNK_ROWS, LANES), f32),
            pltpu.VMEM((chunks, n_depth - 1, pairs, CHUNK_ROWS, LANES), f32),
            pltpu.VMEM((chunks, pairs, CHUNK_ROWS, LANES), f32),
            dma((chunks, n_col - 1)),
            dma((chunks, n_col - 1)),
            dma((n_row // 2 - 1,)),
            dma((n_row // 2 - 1,)),
            dma((n_row // 2,)),
            dma((n_row // 2,)),
            dma((chunks, n_depth - 1)),
            dma((chunks, n_depth - 1)),
            dma(()),
        ],
        compiler_params=pltpu.CompilerParams(
            collective_id=0, has_side_effects=True, vmem_limit_bytes=48 * 1024 * 1024
        ),
        cost_estimate=pl.CostEstimate(
            flops=2 * PC * 4 * order * width * order, bytes_accessed=8 * 1024 * 1024, transcendentals=0
        ),
        name="filtered_product",
    )(left_blocks, right_blocks, triples)


def solution(mesh):
    n_row, n_col, n_depth = mesh.shape["row"], mesh.shape["col"], mesh.shape["depth"]
    devices = n_row * n_col * n_depth
    placed = (
        P(("row", "col", "depth"), None, None),
        P(("row", "col", "depth"), None, None),
        P(None, ("row", "col", "depth")),
    )

    def whole(left_blocks, right_blocks, triples):
        local = left_blocks.shape[0] // devices
        order = left_blocks.shape[1]
        groups = max(1, local // 4)
        sizes = (n_row, n_col, n_depth, order, groups, local // groups, PC // n_depth, order // CHUNK_ROWS)
        return jax.shard_map(
            functools.partial(per_device, sizes),
            mesh=mesh,
            in_specs=placed,
            out_specs=P(("row", "col", "depth"), None, None),
            check_vma=False,
        )(left_blocks, right_blocks, triples)

    return whole
```

time: 358 us -> 47.3 us (0.13)
  waiting for transfers between devices: 183 us -> 0 us
  other arithmetic: 81.2 us -> 0 us
  Pallas kernels: 0 us -> 43 us
  matrix products: 39.3 us -> 0 us
  local copies, waits for them, and re-layouts: 39.7 us -> 4.1 us
  between operations: 13.1 us -> 0.01 us
    psum x1 -> x0, waiting for transfers between devices: 110 us -> none  [per_device(): summed = lax.psum(partial_value, 'depth')]
    scatter-add x4 -> x0, other arithmetic: 80.6 us -> none  [accumulate(): return partial_value.at[out_pick].add(products)]
    all_gather x2 -> x0, waiting for transfers between devices: 71.6 us -> none  [the longest x1 48.7 us: per_device(): left_panel = lax.all_gather(left_blocks, 'col', axis=0, tiled=True)]
    pallas_call x0 -> x1, Pallas kernels: none -> 43 us  [per_device(): pl.pallas_call(functools.partial(kernel, sizes), out_shape=jax.ShapeDtype...]
    dot_general x4 -> x0, matrix products: 39.3 us -> none  [accumulate(): jnp.einsum('tij,tjk->tik', left_panel[left_pick], right_panel[right_pick]...]
    gather x8 -> x0, local copies, waits for them, and re-layouts: 28.5 us -> none  [the longest x4 17.3 us: accumulate(): right_panel[right_pick]]
    slice x2 -> x0, local copies, waits for them, and re-layouts: 5.57 us -> none  [the longest x1 4.75 us: per_device(): partial_value = partial_value[:PC]]
    unnamed x2 -> x7, local copies, waits for them, and re-layouts: 0.01 us -> 4.1 us
  transfers between devices with their start and end apart: 3 -> 0, of which waited for: 3 -> 0; matrix products, arithmetic and copies ran while one was open for 0% -> 0% of each run, Pallas kernels for 0% -> 0%
where the time goes in v1:
time: 47.3 us; the launch traced here: 47.1 us
  Pallas kernels  43 us (91%)
  local copies, waits for them, and re-layouts  4.1 us (9%)
    pallas_call x1, Pallas kernels, per_device(): pl.pallas_call(functools.partial(kernel, sizes), out_shape=jax.ShapeDtype...  43 us
    unnamed x7, local copies, waits for them, and re-layouts  4.1 us

profile of v1, /device:TPU:0, one launch (start us, length us, event | category | flops | bytes accessed | tf_op | source)
XLA Modules:
  0.0 47.1 jit_solution(2192726247755440107)
XLA Ops:
  0.0 0.0 copy-start
  0.0 1.0 %copy-done = f32[16,64,64]{2,1,0:T(8,128)S(1)} copy-done((f32[16,64,64]{2,1,0:T(8,128)S(1)}, f32[16,64,64]{2,1,0:T(8,128)}, u32[]{:S(2)}) %copy-start) | copy-done | bytes 262168
  1.0 0.0 copy-start.1
  1.0 1.0 %copy-done.1 = f32[16,64,64]{2,1,0:T(8,128)S(1)} copy-done((f32[16,64,64]{2,1,0:T(8,128)S(1)}, f32[16,64,64]{2,1,0:T(8,128)}, u32[]{:S(2)}) %copy-start.1) | copy-done | bytes 262168
  2.1 0.0 copy-start.2
  2.1 0.7 %copy-done.2 = s32[3,512]{1,0:T(4,128)S(1)} copy-done((s32[3,512]{1,0:T(4,128)S(1)}, s32[3,512]{1,0:T(4,128)}, u32[]{:S(2)}) %copy-start.2) | copy-done | bytes 6168
  2.8 43.0 %filtered_product.1 = f32[64,64,64]{2,1,0:T(8,128)S(1)} custom-call(f32[16,64,64]{2,1,0:T(8,128)S(1)} %copy-done, f32[16,64,64]{2,1,0:T(8,128)S(1)} %copy-done.1, s32[3,512]{1,0:T(4,128)S(1)} %copy-done.2), custom_call_target="tpu_custom_call" | custom-call | flops 1073741824 | bytes 8388608 | tf_op jit(solution)/shard_map/filtered_product/pallas_call | solution.py:263
  45.7 1.3 %copy.5 = f32[64,64,64]{2,1,0:T(8,128)} copy(f32[64,64,64]{2,1,0:T(8,128)S(1)} %filtered_product.1) | data formatting | bytes 2097152
Async XLA Ops:
  0.0 1.0 %copy-start = (f32[16,64,64]{2,1,0:T(8,128)S(1)}, f32[16,64,64]{2,1,0:T(8,128)}, u32[]{:S(2)}) copy-start(f32[16,64,64]{2,1,0:T(8,128)} %left_ref.1) | copy-start | bytes 786436
  1.0 1.0 %copy-start.1 = (f32[16,64,64]{2,1,0:T(8,128)S(1)}, f32[16,64,64]{2,1,0:T(8,128)}, u32[]{:S(2)}) copy-start(f32[16,64,64]{2,1,0:T(8,128)} %right_ref.1) | copy-start | bytes 786436
  2.1 0.7 %copy-start.2 = (s32[3,512]{1,0:T(4,128)S(1)}, s32[3,512]{1,0:T(4,128)}, u32[]{:S(2)}) copy-start(s32[3,512]{1,0:T(4,128)} %triples_ref.1) | copy-start | bytes 18436

commit v2 on v1

--- a/solution.py
+++ b/solution.py
@@ -10,7 +10,8 @@
 PC = 128
 LANES = 128
 CHUNK_ROWS = 16
-UNROLL_PAIRS = 8
+UNROLL_PAIRS = 4
+HALVES = 2
 MESH = pl.DeviceIdType.MESH
 
 
@@ -22,10 +23,14 @@
 
 def kernel(
     sizes,
+    left_hbm,
+    right_hbm,
+    triples_hbm,
+    out_hbm,
+    out_ref,
     left_ref,
     right_ref,
     triples_ref,
-    out_ref,
     left_all,
     right_all,
     right_split,
@@ -46,6 +51,8 @@
     part_send_sem,
     part_recv_sem,
     code_sem,
+    in_sem,
+    out_sem,
 ):
     n_row, n_col, n_depth, order, groups, local_rows, share, chunks = sizes
     row = lax.axis_index("row")
@@ -61,6 +68,15 @@
     def turn(index, step, count):
         return lax.rem(index + step, count)
 
+    fetches = [
+        pltpu.make_async_copy(source, target, in_sem.at[n])
+        for n, (source, target) in enumerate(
+            ((right_hbm, right_ref), (left_hbm, left_ref), (triples_hbm, triples_ref))
+        )
+    ]
+    for fetch in fetches:
+        fetch.start()
+
     barrier = pltpu.get_barrier_semaphore()
     greeted = 0
     for step in range(1, n_col):
@@ -77,15 +93,17 @@
         pl.semaphore_signal(barrier, inc=1, device_id={"depth": turn(depth, step, n_depth)}, device_id_type=MESH)
         greeted += 1
 
+    fetches[0].wait()
+    for j in range(0, local_rows, 2):
+        for g in range(groups):
+            pair = jnp.concatenate([right_ref[j * groups + g], right_ref[(j + 1) * groups + g]], axis=-1)
+            right_all[row, j // 2, g * order : (g + 1) * order, :] = pair
+    fetches[1].wait()
     for i in range(local_rows):
         for g in range(0, groups, 2):
             pair = jnp.concatenate([left_ref[i * groups + g], left_ref[i * groups + g + 1]], axis=-1)
             for q in range(chunks):
                 left_all[q, col, i, :, g * order : (g + 2) * order] = pair[q * CHUNK_ROWS : (q + 1) * CHUNK_ROWS]
-    for j in range(0, local_rows, 2):
-        for g in range(groups):
-            pair = jnp.concatenate([right_ref[j * groups + g], right_ref[(j + 1) * groups + g]], axis=-1)
-            right_all[row, j // 2, g * order : (g + 1) * order, :] = pair
 
     pl.semaphore_wait(barrier, greeted)
 
@@ -120,12 +138,13 @@
             device_id_type=MESH,
         )
 
-    def part_copy(q, step):
+    def part_copy(q, step, half):
+        piece = pl.ds(half * (pairs // HALVES), pairs // HALVES)
         return pltpu.make_async_remote_copy(
-            src_ref=part_send.at[q, step - 1],
-            dst_ref=part_recv.at[q, step - 1],
-            send_sem=part_send_sem.at[q, step - 1],
-            recv_sem=part_recv_sem.at[q, step - 1],
+            src_ref=part_send.at[q, step - 1, piece],
+            dst_ref=part_recv.at[q, step - 1, piece],
+            send_sem=part_send_sem.at[q, step - 1, half],
+            recv_sem=part_recv_sem.at[q, step - 1, half],
             device_id={"depth": turn(depth, step, n_depth)},
             device_id_type=MESH,
         )
@@ -139,16 +158,20 @@
         for step in range(n_col - 1, 0, -1):
             left_copy(q, step).start()
 
+    fetches[2].wait()
     left_slot = triples_ref[0:1, :]
     right_slot = triples_ref[1:2, :]
     out_slot = triples_ref[2:3, :]
     group_of = lax.rem(left_slot, groups)
-    code = lax.div(left_slot, groups) * 1024 + lax.div(right_slot, groups)
+    block_row = lax.div(left_slot, groups)
+    block_col = lax.div(right_slot, groups)
+    code_lane = lax.broadcasted_iota(jnp.int32, (16, LANES), 1)
     lane = lax.broadcasted_iota(jnp.int32, (16, width), 1)
     for k in range(0, PC, 16):
         here = out_slot == lax.broadcasted_iota(jnp.int32, (16, out_slot.shape[1]), 0) + k
-        found = jnp.max(jnp.where(here, code, 0), axis=1, keepdims=True)
-        code_rows[k : k + 16, :] = jnp.broadcast_to(found, (16, LANES))
+        at_row = jnp.max(jnp.where(here, block_row, 0), axis=1, keepdims=True)
+        at_col = jnp.max(jnp.where(here, block_col, 0), axis=1, keepdims=True)
+        code_rows[k : k + 16, :] = jnp.where(code_lane == 0, at_row, at_col)
         used = jnp.zeros((16, width), jnp.float32)
         for g in range(groups):
             at_group = jnp.max(
@@ -193,15 +216,14 @@
     lane_low = lax.broadcasted_iota(jnp.int32, (CHUNK_ROWS, LANES), 1) < order
 
     def one_slot(q, k):
-        found = codes[k, 0]
-        picked = left_split[q, found // 1024]
+        picked = left_split[q, codes[k, 0]]
         used = mask_ref[k]
         picked = picked * jnp.concatenate([used, used], axis=0)
-        both = jnp.dot(picked, right_split[found % 1024], preferred_element_type=jnp.float32)
+        both = jnp.dot(picked, right_split[codes[k, 1]], preferred_element_type=jnp.float32)
         both = both[:CHUNK_ROWS] + both[CHUNK_ROWS:]
         return both + pltpu.roll(both, order, 1)
 
-    def products(q, first, target):
+    def products(q, first, target, half):
         def body(turn_index, carry):
             for inner in range(UNROLL_PAIRS):
                 p = turn_index * UNROLL_PAIRS + inner
@@ -209,11 +231,17 @@
                 target[p] = jnp.where(lane_low, one_slot(q, k), one_slot(q, k + 1))
             return carry
 
-        lax.fori_loop(0, pairs // UNROLL_PAIRS, body, 0)
+        turns = pairs // UNROLL_PAIRS // HALVES
+        lax.fori_loop(half * turns, (half + 1) * turns, body, 0)
+
+    def out_copy(q):
+        rows = pl.ds(q * CHUNK_ROWS, CHUNK_ROWS)
+        return pltpu.make_async_copy(out_ref.at[:, rows, :], out_hbm.at[:, rows, :], out_sem.at[q])
 
     def finish(q):
         for step in range(1, n_depth):
-            part_copy(q, step).wait_recv()
+            for half in range(HALVES):
+                part_copy(q, step, half).wait_recv()
 
         def body(p, carry):
             total = part_own[q, p]
@@ -225,6 +253,7 @@
             return carry
 
         lax.fori_loop(0, pairs, body, 0, unroll=min(8, pairs))
+        out_copy(q).start()
 
     for q in range(chunks):
         for step in range(1, n_col):
@@ -236,18 +265,22 @@
                 left_split[q, shard * local_rows + i, CHUNK_ROWS:, :] = low
         for step in range(1, n_depth):
             partner = turn(depth, step, n_depth)
-            products(q, partner * share, part_send.at[q, step - 1])
-            part_copy(q, step).start()
-        products(q, depth * share, part_own.at[q])
+            for half in range(HALVES):
+                products(q, partner * share, part_send.at[q, step - 1], half)
+                part_copy(q, step, half).start()
+        for half in range(HALVES):
+            products(q, depth * share, part_own.at[q], half)
         if q > 0:
             finish(q - 1)
     finish(chunks - 1)
 
     for q in range(chunks):
+        out_copy(q).wait()
         for step in range(1, n_col):
             left_copy(q, step).wait_send()
         for step in range(1, n_depth):
-            part_copy(q, step).wait_send()
+            for half in range(HALVES):
+                part_copy(q, step, half).wait_send()
     for step in range(1, outers):
         right_copy(step).wait_send()
     for step in range(outers):
@@ -263,9 +296,13 @@
     return pl.pallas_call(
         functools.partial(kernel, sizes),
         out_shape=jax.ShapeDtypeStruct((share, order, order), f32),
-        in_specs=[pl.BlockSpec(memory_space=pltpu.VMEM)] * 3,
-        out_specs=pl.BlockSpec(memory_space=pltpu.VMEM),
+        in_specs=[pl.BlockSpec(memory_space=pl.ANY)] * 3,
+        out_specs=pl.BlockSpec(memory_space=pl.ANY),
         scratch_shapes=[
+            pltpu.VMEM((share, order, order), f32),
+            pltpu.VMEM(left_blocks.shape, f32),
+            pltpu.VMEM(right_blocks.shape, f32),
+            pltpu.VMEM(triples.shape, i32),
             pltpu.VMEM((chunks, n_col, local_rows, CHUNK_ROWS, width), f32),
             pltpu.VMEM((n_row, local_rows // 2, width, LANES), f32),
             pltpu.VMEM((n_row * local_rows, width, LANES), bf16),
@@ -283,12 +320,14 @@
             dma((n_row // 2 - 1,)),
             dma((n_row // 2,)),
             dma((n_row // 2,)),
-            dma((chunks, n_depth - 1)),
-            dma((chunks, n_depth - 1)),
+            dma((chunks, n_depth - 1, HALVES)),
+            dma((chunks, n_depth - 1, HALVES)),
             dma(()),
+            dma((3,)),
+            dma((chunks,)),
         ],
         compiler_params=pltpu.CompilerParams(
-            collective_id=0, has_side_effects=True, vmem_limit_bytes=48 * 1024 * 1024
+            collective_id=0, has_side_effects=True, vmem_limit_bytes=60 * 1024 * 1024
         ),
         cost_estimate=pl.CostEstimate(
             flops=2 * PC * 4 * order * width * order, bytes_accessed=8 * 1024 * 1024, transcendentals=0

time: 47.3 us -> 47 us (level)
  local copies, waits for them, and re-layouts: 4.1 us -> 3.16 us
  Pallas kernels: 43 us -> 43.7 us
    unnamed x7 -> x1, local copies, waits for them, and re-layouts: 4.1 us -> 3.16 us
    pallas_call x1, Pallas kernels: 43 us -> 43.7 us  [per_device(): pl.pallas_call(functools.partial(kernel, sizes), out_shape=jax.ShapeDtype...]
where the time goes in v2:
time: 47 us; the launch traced here: 46.9 us
  Pallas kernels  43.7 us (93%)
  local copies, waits for them, and re-layouts  3.16 us (7%)
    pallas_call x1, Pallas kernels, per_device(): pl.pallas_call(functools.partial(kernel, sizes), out_shape=jax.ShapeDtype...  43.7 us
    unnamed x1, local copies, waits for them, and re-layouts  3.16 us

profile of v2, /device:TPU:0, one launch (start us, length us, event | category | flops | bytes accessed | tf_op | source)
XLA Modules:
  0.0 46.9 jit_solution(10326368504841580374)
XLA Ops:
  0.0 43.7 %filtered_product.1 = f32[64,64,64]{2,1,0:T(8,128)} custom-call(f32[16,64,64]{2,1,0:T(8,128)} %left_hbm.1, f32[16,64,64]{2,1,0:T(8,128)} %right_hbm.1, s32[3,512]{1,0:T(4,128)} %triples_hbm.1), custom_call_target="tpu_custom_call" | custom-call | flops 1073741824 | bytes 8388608 | tf_op jit(solution)/shard_map/filtered_product/pallas_call | solution.py:296
  43.7 3.2 %copy.5 = f32[64,64,64]{2,1,0:T(8,128)} copy(f32[64,64,64]{2,1,0:T(8,128)} %filtered_product.1) | data formatting | bytes 2097152

commit v3 on v2

--- a/solution.py
+++ b/solution.py
@@ -1,4 +1,5 @@
 import functools
+import math
 
 import jax
 import jax.numpy as jnp
@@ -9,7 +10,7 @@
 
 PC = 128
 LANES = 128
-CHUNK_ROWS = 16
+CHUNK_ROWS = 32
 UNROLL_PAIRS = 4
 HALVES = 2
 MESH = pl.DeviceIdType.MESH
@@ -248,8 +249,7 @@
             for step in range(1, n_depth):
                 total = total + part_recv[q, step - 1, p]
             rows = pl.ds(q * CHUNK_ROWS, CHUNK_ROWS)
-            out_ref[2 * p, rows, :] = total[:, :order]
-            out_ref[2 * p + 1, rows, :] = pltpu.roll(total, order, 1)[:, :order]
+            out_ref[p, rows, :] = total
             return carry
 
         lax.fori_loop(0, pairs, body, 0, unroll=min(8, pairs))
@@ -287,19 +287,27 @@
         core_copy(step).wait_send()
 
 
+def unpack(packed_ref, kept_ref):
+    order = kept_ref.shape[1]
+    for p in range(packed_ref.shape[0]):
+        pair = packed_ref[p]
+        kept_ref[2 * p] = pair[:, :order]
+        kept_ref[2 * p + 1] = pltpu.roll(pair, order, 1)[:, :order]
+
+
 def per_device(sizes, left_blocks, right_blocks, triples):
     n_row, n_col, n_depth, order, groups, local_rows, share, chunks = sizes
     width = groups * order
     pairs = share // 2
     f32, bf16, i32 = jnp.float32, jnp.bfloat16, jnp.int32
     dma = pltpu.SemaphoreType.DMA
-    return pl.pallas_call(
+    packed = pl.pallas_call(
         functools.partial(kernel, sizes),
-        out_shape=jax.ShapeDtypeStruct((share, order, order), f32),
+        out_shape=jax.ShapeDtypeStruct((pairs, order, LANES), f32),
         in_specs=[pl.BlockSpec(memory_space=pl.ANY)] * 3,
         out_specs=pl.BlockSpec(memory_space=pl.ANY),
         scratch_shapes=[
-            pltpu.VMEM((share, order, order), f32),
+            pltpu.VMEM((pairs, order, LANES), f32),
             pltpu.VMEM(left_blocks.shape, f32),
             pltpu.VMEM(right_blocks.shape, f32),
             pltpu.VMEM(triples.shape, i32),
@@ -334,6 +342,15 @@
         ),
         name="filtered_product",
     )(left_blocks, right_blocks, triples)
+    steps = math.gcd(pairs, 4)
+    return pl.pallas_call(
+        unpack,
+        out_shape=jax.ShapeDtypeStruct((share, order, order), f32),
+        grid=(steps,),
+        in_specs=[pl.BlockSpec((pairs // steps, order, LANES), lambda n: (n, 0, 0))],
+        out_specs=pl.BlockSpec((share // steps, order, order), lambda n: (n, 0, 0)),
+        name="unpack_blocks",
+    )(packed)
 
 
 def solution(mesh):

time: 47 us -> 50.4 us (1.072)
  the two profiles are of different devices: /device:TPU:0 before, /device:TPU:16 now
where the time goes in v3:
time: 50.4 us; the launch traced here: 50.2 us
  Pallas kernels  50.2 us (100%)
    pallas_call x1, Pallas kernels, per_device(): pl.pallas_call(functools.partial(kernel, sizes), out_shape=jax.ShapeDtype...  46.4 us
    pallas_call x1, Pallas kernels, per_device(): pl.pallas_call(unpack, out_shape=jax.ShapeDtypeStruct((share, order, orde...  3.79 us

profile of v3, /device:TPU:16, one launch (start us, length us, event | category | flops | bytes accessed | tf_op | source)
XLA Modules:
  0.0 50.2 jit_solution(262178921805244025)
XLA Ops:
  0.0 46.4 %filtered_product.1.packed_ref = f32[32,64,128]{2,1,0:T(8,128)} custom-call(f32[16,64,64]{2,1,0:T(8,128)} %left_hbm.1, f32[16,64,64]{2,1,0:T(8,128)} %right_hbm.1, s32[3,512]{1,0:T(4,128)} %triples_hbm.1), custom_call_target="tpu_custom_call" | custom-call | flops 1073741824 | bytes 8388608 | tf_op jit(solution)/shard_map/filtered_product/pallas_call | solution.py:304
  46.5 3.8 %unpack_blocks.1 = f32[64,64,64]{2,1,0:T(8,128)} custom-call(f32[32,64,128]{2,1,0:T(8,128)} %filtered_product.1.packed_ref), custom_call_target="tpu_custom_call" | custom-call | tf_op jit(solution)/shard_map/unpack_blocks/pallas_call | solution.py:346

commit v4 on v2

--- a/solution.py
+++ b/solution.py
@@ -26,7 +26,6 @@
     left_hbm,
     right_hbm,
     triples_hbm,
-    out_hbm,
     out_ref,
     left_ref,
     right_ref,
@@ -52,7 +51,6 @@
     part_recv_sem,
     code_sem,
     in_sem,
-    out_sem,
 ):
     n_row, n_col, n_depth, order, groups, local_rows, share, chunks = sizes
     row = lax.axis_index("row")
@@ -107,15 +105,38 @@
 
     pl.semaphore_wait(barrier, greeted)
 
-    def left_copy(q, step):
+    def left_copy(q, shard, way, hops):
         return pltpu.make_async_remote_copy(
-            src_ref=left_all.at[q, col],
-            dst_ref=left_all.at[q, col],
-            send_sem=left_send_sem.at[q, step - 1],
-            recv_sem=left_recv_sem.at[q, step - 1],
-            device_id={"col": turn(col, step, n_col)},
+            src_ref=left_all.at[q, shard],
+            dst_ref=left_all.at[q, shard],
+            send_sem=left_send_sem.at[q, max(way, 0), hops],
+            recv_sem=left_recv_sem.at[q, max(way, 0), hops],
+            device_id={"col": turn(col + n_col, way, n_col)},
             device_id_type=MESH,
         )
+
+    def along(way, hops, act):
+        shard = col - way * hops
+        ahead = col + way
+        held = jnp.logical_and(shard >= 0, shard < n_col)
+
+        @pl.when(jnp.logical_and(held, jnp.logical_and(ahead >= 0, ahead < n_col)))
+        def _():
+            act(shard)
+
+    def left_start(q, hops):
+        for way in (1, -1):
+            along(way, hops, lambda shard: left_copy(q, shard, way, hops).start())
+
+    def left_arrive(q, hops):
+        for way in (1, -1):
+            shard = col - way * hops
+
+            @pl.when(jnp.logical_and(shard >= 0, shard < n_col))
+            def _():
+                left_copy(q, shard, way, hops - 1).wait_recv()
+
+            along(way, hops, lambda shard: left_copy(q, shard, way, hops).start())
 
     def right_copy(step):
         return pltpu.make_async_remote_copy(
@@ -151,12 +172,10 @@
 
     for step in range(1, outers):
         right_copy(step).start()
-    for step in range(n_col - 1, 0, -1):
-        left_copy(0, step).start()
+    left_start(0, 0)
     core_copy(0).start()
-    for q in range(1, chunks):
-        for step in range(n_col - 1, 0, -1):
-            left_copy(q, step).start()
+    if chunks > 1:
+        left_start(1, 0)
 
     fetches[2].wait()
     left_slot = triples_ref[0:1, :]
@@ -202,6 +221,8 @@
                 right_split[at, rows, :] = jnp.where(lower, high, low).astype(jnp.bfloat16)
                 right_split[at + 1, rows, :] = jnp.where(lower, low, high).astype(jnp.bfloat16)
 
+    for hops in range(1, n_col - 1):
+        left_arrive(0, hops)
     split_right(row)
     core_copy(0).wait_recv()
     split_right(other_core)
@@ -233,10 +254,6 @@
 
         turns = pairs // UNROLL_PAIRS // HALVES
         lax.fori_loop(half * turns, (half + 1) * turns, body, 0)
-
-    def out_copy(q):
-        rows = pl.ds(q * CHUNK_ROWS, CHUNK_ROWS)
-        return pltpu.make_async_copy(out_ref.at[:, rows, :], out_hbm.at[:, rows, :], out_sem.at[q])
 
     def finish(q):
         for step in range(1, n_depth):
@@ -253,11 +270,11 @@
             return carry
 
         lax.fori_loop(0, pairs, body, 0, unroll=min(8, pairs))
-        out_copy(q).start()
 
     for q in range(chunks):
-        for step in range(1, n_col):
-            left_copy(q, step).wait_recv()
+        left_arrive(q, n_col - 1)
+        if q + 2 < chunks:
+            left_start(q + 2, 0)
         for shard in range(n_col):
             for i in range(local_rows):
                 high, low = split_bf16(left_all[q, shard, i])
@@ -268,16 +285,19 @@
             for half in range(HALVES):
                 products(q, partner * share, part_send.at[q, step - 1], half)
                 part_copy(q, step, half).start()
+        hops_ahead = range(1, n_col - 1) if q + 1 < chunks else range(0)
         for half in range(HALVES):
+            for hops in hops_ahead[half::HALVES]:
+                left_arrive(q + 1, hops)
             products(q, depth * share, part_own.at[q], half)
         if q > 0:
             finish(q - 1)
     finish(chunks - 1)
 
     for q in range(chunks):
-        out_copy(q).wait()
-        for step in range(1, n_col):
-            left_copy(q, step).wait_send()
+        for hops in range(n_col - 1):
+            for way in (1, -1):
+                along(way, hops, lambda shard: left_copy(q, shard, way, hops).wait_send())
         for step in range(1, n_depth):
             for half in range(HALVES):
                 part_copy(q, step, half).wait_send()
@@ -297,9 +317,8 @@
         functools.partial(kernel, sizes),
         out_shape=jax.ShapeDtypeStruct((share, order, order), f32),
         in_specs=[pl.BlockSpec(memory_space=pl.ANY)] * 3,
-        out_specs=pl.BlockSpec(memory_space=pl.ANY),
+        out_specs=pl.BlockSpec(memory_space=pltpu.VMEM),
         scratch_shapes=[
-            pltpu.VMEM((share, order, order), f32),
             pltpu.VMEM(left_blocks.shape, f32),
             pltpu.VMEM(right_blocks.shape, f32),
             pltpu.VMEM(triples.shape, i32),
@@ -314,8 +333,8 @@
             pltpu.VMEM((chunks, n_depth - 1, pairs, CHUNK_ROWS, LANES), f32),
             pltpu.VMEM((chunks, n_depth - 1, pairs, CHUNK_ROWS, LANES), f32),
             pltpu.VMEM((chunks, pairs, CHUNK_ROWS, LANES), f32),
-            dma((chunks, n_col - 1)),
-            dma((chunks, n_col - 1)),
+            dma((chunks, 2, n_col - 1)),
+            dma((chunks, 2, n_col - 1)),
             dma((n_row // 2 - 1,)),
             dma((n_row // 2 - 1,)),
             dma((n_row // 2,)),
@@ -324,16 +343,15 @@
             dma((chunks, n_depth - 1, HALVES)),
             dma(()),
             dma((3,)),
-            dma((chunks,)),
         ],
         compiler_params=pltpu.CompilerParams(
-            collective_id=0, has_side_effects=True, vmem_limit_bytes=60 * 1024 * 1024
+            collective_id=0, has_side_effects=True, vmem_limit_bytes=48 * 1024 * 1024
         ),
         cost_estimate=pl.CostEstimate(
             flops=2 * PC * 4 * order * width * order, bytes_accessed=8 * 1024 * 1024, transcendentals=0
         ),
         name="filtered_product",
-    )(left_blocks, right_blocks, triples)
+    )(*(pltpu.with_memory_space_constraint(x, pltpu.HBM) for x in (left_blocks, right_blocks, triples)))
 
 
 def solution(mesh):

time: 47 us -> 46.4 us (0.987)
  local copies, waits for them, and re-layouts: 3.16 us -> 1.32 us
  Pallas kernels: 43.7 us -> 44.9 us
    unnamed x1, local copies, waits for them, and re-layouts: 3.16 us -> 1.32 us
    pallas_call x1, Pallas kernels: 43.7 us -> 44.9 us  [per_device(): pl.pallas_call(functools.partial(kernel, sizes), out_shape=jax.ShapeDtype...]
where the time goes in v4:
time: 46.4 us; the launch traced here: 46.2 us
  Pallas kernels  44.9 us (97%)
  local copies, waits for them, and re-layouts  1.32 us (3%)
    pallas_call x1, Pallas kernels, per_device(): pl.pallas_call(functools.partial(kernel, sizes), out_shape=jax.ShapeDtype...  44.9 us
    unnamed x1, local copies, waits for them, and re-layouts  1.32 us

profile of v4, /device:TPU:0, one launch (start us, length us, event | category | flops | bytes accessed | tf_op | source)
XLA Modules:
  0.0 46.2 jit_solution(12938821928831635006)
XLA Ops:
  0.0 44.9 %filtered_product.1 = f32[64,64,64]{2,1,0:T(8,128)S(1)} custom-call(f32[16,64,64]{2,1,0:T(8,128)} %left_hbm.1, f32[16,64,64]{2,1,0:T(8,128)} %right_hbm.1, s32[3,512]{1,0:T(4,128)} %triples_hbm.1), custom_call_target="tpu_custom_call" | custom-call | flops 1073741824 | bytes 8388608 | tf_op jit(solution)/shard_map/filtered_product/pallas_call | solution.py:316
  44.9 1.3 %copy.5 = f32[64,64,64]{2,1,0:T(8,128)} copy(f32[64,64,64]{2,1,0:T(8,128)S(1)} %filtered_product.1) | data formatting | bytes 2097152

commit v5 on v4

v5 whole, which is shorter than its diff:
```python
import functools

import jax
import jax.numpy as jnp
from jax import lax
from jax.experimental import pallas as pl
from jax.experimental.pallas import tpu as pltpu
from jax.sharding import PartitionSpec as P

PC = 128
LANES = 128
CHUNK_ROWS = 16
UNROLL_PAIRS = 4
HALVES = 2
HYBRID = 1
MESH = pl.DeviceIdType.MESH


def split_bf16(value):
    high = value.astype(jnp.bfloat16)
    low = (value - high.astype(jnp.float32)).astype(jnp.bfloat16)
    return high, low


def kernel(
    sizes,
    left_hbm,
    right_hbm,
    triples_hbm,
    out_ref,
    left_ref,
    right_ref,
    triples_both,
    left_all,
    right_all,
    right_split,
    left_split,
    mask_ref,
    mask_rows,
    code_rows,
    codes,
    part_send,
    part_recv,
    part_own,
    left_send_sem,
    left_recv_sem,
    right_send_sem,
    right_recv_sem,
    core_send_sem,
    core_recv_sem,
    part_send_sem,
    part_recv_sem,
    code_sem,
    in_sem,
    layer_send_sem,
    layer_recv_sem,
):
    n_row, n_col, n_depth, order, groups, local_rows, share, chunks, hybrid = sizes
    row = lax.axis_index("row")
    col = lax.axis_index("col")
    depth = lax.axis_index("depth")
    outers = n_row // 2
    core = row % 2
    outer = row // 2
    other_core = outer * 2 + (1 - core)
    width = groups * order
    pairs = share // 2

    def turn(index, step, count):
        return lax.rem(index + step, count)

    fetches = [
        pltpu.make_async_copy(source, target, in_sem.at[n])
        for n, (source, target) in enumerate(
            ((right_hbm, right_ref), (left_hbm, left_ref), (triples_hbm, triples_both.at[0]))
        )
    ]
    for fetch in fetches:
        fetch.start()

    barrier = pltpu.get_barrier_semaphore()
    greeted = 0
    for step in range(1, n_col):
        pl.semaphore_signal(barrier, inc=1, device_id={"col": turn(col, step, n_col)}, device_id_type=MESH)
        greeted += 1
    for step in range(1, outers):
        pl.semaphore_signal(
            barrier, inc=1, device_id={"row": turn(outer, step, outers) * 2 + core}, device_id_type=MESH
        )
        greeted += 1
    pl.semaphore_signal(barrier, inc=1, device_id={"row": other_core}, device_id_type=MESH)
    greeted += 1
    for step in range(1, n_depth):
        pl.semaphore_signal(barrier, inc=1, device_id={"depth": turn(depth, step, n_depth)}, device_id_type=MESH)
        greeted += 1

    fetches[0].wait()
    for j in range(0, local_rows, 2):
        for g in range(groups):
            pair = jnp.concatenate([right_ref[j * groups + g], right_ref[(j + 1) * groups + g]], axis=-1)
            right_all[0, row, j // 2, g * order : (g + 1) * order, :] = pair
    fetches[1].wait()
    for i in range(local_rows):
        for g in range(0, groups, 2):
            pair = jnp.concatenate([left_ref[i * groups + g], left_ref[i * groups + g + 1]], axis=-1)
            for q in range(chunks):
                left_all[q, col, i, :, g * order : (g + 2) * order] = pair[q * CHUNK_ROWS : (q + 1) * CHUNK_ROWS]

    pl.semaphore_wait(barrier, greeted)

    def left_copy(q, shard, way, hops):
        return pltpu.make_async_remote_copy(
            src_ref=left_all.at[q, shard],
            dst_ref=left_all.at[q, shard],
            send_sem=left_send_sem.at[q, max(way, 0), hops],
            recv_sem=left_recv_sem.at[q, max(way, 0), hops],
            device_id={"col": turn(col + n_col, way, n_col)},
            device_id_type=MESH,
        )

    def along(way, hops, act):
        shard = col - way * hops
        ahead = col + way
        held = jnp.logical_and(shard >= 0, shard < n_col)

        @pl.when(jnp.logical_and(held, jnp.logical_and(ahead >= 0, ahead < n_col)))
        def _():
            act(shard)

    def left_start(q, hops):
        for way in (1, -1):
            along(way, hops, lambda shard: left_copy(q, shard, way, hops).start())

    def left_arrive(q, hops):
        for way in (1, -1):
            shard = col - way * hops

            @pl.when(jnp.logical_and(shard >= 0, shard < n_col))
            def _():
                left_copy(q, shard, way, hops - 1).wait_recv()

            along(way, hops, lambda shard: left_copy(q, shard, way, hops).start())

    def right_copy(layer, step):
        return pltpu.make_async_remote_copy(
            src_ref=right_all.at[layer, row],
            dst_ref=right_all.at[layer, row],
            send_sem=right_send_sem.at[layer, step - 1],
            recv_sem=right_recv_sem.at[layer, step - 1],
            device_id={"row": turn(outer, step, outers) * 2 + core},
            device_id_type=MESH,
        )

    def core_copy(layer, step):
        source = turn(outer + outers, -step, outers) * 2 + core
        return pltpu.make_async_remote_copy(
            src_ref=right_all.at[layer, source],
            dst_ref=right_all.at[layer, source],
            send_sem=core_send_sem.at[layer, step],
            recv_sem=core_recv_sem.at[layer, step],
            device_id={"row": other_core},
            device_id_type=MESH,
        )

    def layer_copy(n):
        if n == 0:
            source, target = triples_both.at[0], triples_both.at[1]
        elif n == 1:
            source, target = right_all.at[0, row], right_all.at[1, row]
        else:
            source, target = left_all.at[chunks - hybrid + n - 2, col], left_all.at[chunks + n - 2, col]
        return pltpu.make_async_remote_copy(
            src_ref=source,
            dst_ref=target,
            send_sem=layer_send_sem.at[n],
            recv_sem=layer_recv_sem.at[n],
            device_id={"depth": turn(depth, 1, n_depth)},
            device_id_type=MESH,
        )

    def chunk_parts(q):
        return [q] if q < chunks - hybrid else [q, q + hybrid]

    def begin(q):
        for part in chunk_parts(q):
            if part >= chunks:
                layer_copy(part - chunks + 2).wait_recv()
            left_start(part, 0)

    def part_copy(q, step, half):
        piece = pl.ds(half * (pairs // HALVES), pairs // HALVES)
        return pltpu.make_async_remote_copy(
            src_ref=part_send.at[q, step - 1, piece],
            dst_ref=part_recv.at[q, step - 1, piece],
            send_sem=part_send_sem.at[q, step - 1, half],
            recv_sem=part_recv_sem.at[q, step - 1, half],
            device_id={"depth": turn(depth, step, n_depth)},
            device_id_type=MESH,
        )

    for step in range(1, outers):
        right_copy(0, step).start()
    left_start(0, 0)
    core_copy(0, 0).start()
    fetches[2].wait()
    layers = 2 if hybrid else 1
    if hybrid:
        for n in range(hybrid + 2):
            layer_copy(n).start()
    begin(1)

    lane = lax.broadcasted_iota(jnp.int32, (16, width), 1)
    code_lane = lax.broadcasted_iota(jnp.int32, (16, LANES), 1)

    def tabulate(layer):
        left_slot = triples_both[layer, 0:1, :]
        right_slot = triples_both[layer, 1:2, :]
        out_slot = triples_both[layer, 2:3, :]
        group_of = lax.rem(left_slot, groups)
        block_row = lax.div(left_slot, groups)
        block_col = lax.div(right_slot, groups)
        for k in range(0, PC, 16):
            here = out_slot == lax.broadcasted_iota(jnp.int32, (16, out_slot.shape[1]), 0) + k
            at_row = jnp.max(jnp.where(here, block_row, 0), axis=1, keepdims=True)
            at_col = jnp.max(jnp.where(here, block_col, 0), axis=1, keepdims=True)
            code_rows[layer, k : k + 16, :] = jnp.where(code_lane == 0, at_row, at_col)
            used = jnp.zeros((16, width), jnp.float32)
            for g in range(groups):
                at_group = jnp.max(
                    jnp.where(here & (group_of == g), 1.0, 0.0).astype(jnp.float32), axis=1, keepdims=True
                )
                used = jnp.where(lane // order == g, at_group, used)
            mask_rows[layer, k : k + 16, :] = used
        code_copy = pltpu.make_async_copy(code_rows.at[layer], codes.at[layer], code_sem.at[layer])
        code_copy.start()

        def spread(k, carry):
            mask_ref[layer, k] = jnp.broadcast_to(
                mask_rows[layer, pl.ds(k, 1), :], (CHUNK_ROWS, width)
            ).astype(jnp.bfloat16)
            return carry

        lax.fori_loop(0, PC, spread, 0, unroll=8)
        code_copy.wait()

    tabulate(0)
    if hybrid:
        layer_copy(0).wait_recv()
        tabulate(1)

    lower = lax.broadcasted_iota(jnp.int32, (order, LANES), 1) < order

    def split_right(layer, shard):
        for j in range(local_rows // 2):
            for g in range(groups):
                rows = slice(g * order, (g + 1) * order)
                value = right_all[layer, shard, j, rows, :]
                high = value.astype(jnp.bfloat16).astype(jnp.float32)
                low = pltpu.roll(value - high, order, 1)
                at = shard * local_rows + 2 * j
                right_split[layer, at, rows, :] = jnp.where(lower, high, low).astype(jnp.bfloat16)
                right_split[layer, at + 1, rows, :] = jnp.where(lower, low, high).astype(jnp.bfloat16)

    for hops in range(1, n_col - 1):
        left_arrive(0, hops)
    split_right(0, row)
    core_copy(0, 0).wait_recv()
    split_right(0, other_core)

    def right_pass(layer, split):
        for step in range(1, outers):
            right_copy(layer, step).wait_recv()
            core_copy(layer, step).start()
            if split:
                split_right(layer, turn(outer + outers, -step, outers) * 2 + core)

    def right_last(layer):
        for step in range(1, outers):
            core_copy(layer, step).wait_recv()
            split_right(layer, turn(outer + outers, -step, outers) * 2 + (1 - core))

    right_pass(0, True)
    if hybrid:
        layer_copy(1).wait_recv()
        for step in range(1, outers):
            right_copy(1, step).start()
        core_copy(1, 0).start()
    right_last(0)

    lane_low = lax.broadcasted_iota(jnp.int32, (CHUNK_ROWS, LANES), 1) < order

    def one_slot(layer, q, k):
        picked = left_split[q, codes[layer, k, 0]]
        used = mask_ref[layer, k]
        picked = picked * jnp.concatenate([used, used], axis=0)
        both = jnp.dot(picked, right_split[layer, codes[layer, k, 1]], preferred_element_type=jnp.float32)
        both = both[:CHUNK_ROWS] + both[CHUNK_ROWS:]
        return both + pltpu.roll(both, order, 1)

    def products(parts, first, target, half):
        def body(turn_index, carry):
            for inner in range(UNROLL_PAIRS):
                p = turn_index * UNROLL_PAIRS + inner
                k = first + 2 * p
                total = None
                for layer, part in enumerate(parts):
                    pair = jnp.where(lane_low, one_slot(layer, part, k), one_slot(layer, part, k + 1))
                    total = pair if total is None else total + pair
                target[p] = total
            return carry

        turns = pairs // UNROLL_PAIRS // HALVES
        lax.fori_loop(half * turns, (half + 1) * turns, body, 0)

    def finish(q):
        sent = range(1, n_depth) if q < chunks - hybrid else range(0)
        for step in sent:
            for half in range(HALVES):
                part_copy(q, step, half).wait_recv()

        def body(p, carry):
            total = part_own[q, p]
            for step in sent:
                total = total + part_recv[q, step - 1, p]
            rows = pl.ds(q * CHUNK_ROWS, CHUNK_ROWS)
            out_ref[2 * p, rows, :] = total[:, :order]
            out_ref[2 * p + 1, rows, :] = pltpu.roll(total, order, 1)[:, :order]
            return carry

        lax.fori_loop(0, pairs, body, 0, unroll=min(8, pairs))

    for q in range(chunks):
        for part in chunk_parts(q):
            left_arrive(part, n_col - 1)
        if q + 2 < chunks:
            begin(q + 2)
        for part in chunk_parts(q):
            for shard in range(n_col):
                for i in range(local_rows):
                    high, low = split_bf16(left_all[part, shard, i])
                    left_split[part, shard * local_rows + i, :CHUNK_ROWS, :] = high
                    left_split[part, shard * local_rows + i, CHUNK_ROWS:, :] = low
        if q < chunks - hybrid:
            for step in range(1, n_depth):
                partner = turn(depth, step, n_depth)
                for half in range(HALVES):
                    products([q], partner * share, part_send.at[q, step - 1], half)
                    part_copy(q, step, half).start()
        hops_ahead = range(1, n_col - 1) if q + 1 < chunks else range(0)
        for half in range(HALVES):
            for hops in hops_ahead[half::HALVES]:
                for part in chunk_parts(q + 1):
                    left_arrive(part, hops)
            products(chunk_parts(q), depth * share, part_own.at[q], half)
        if hybrid and q == 0:
            right_pass(1, False)
        if hybrid and q == 1:
            core_copy(1, 0).wait_recv()
            right_last(1)
            split_right(1, row)
            split_right(1, other_core)
            for step in range(1, outers):
                split_right(1, turn(outer + outers, -step, outers) * 2 + core)
        if q > 0 and q < chunks - hybrid:
            finish(q - 1)
    for q in range(max(0, chunks - hybrid - 1), chunks):
        finish(q)

    for q in range(chunks):
        for part in chunk_parts(q):
            for hops in range(n_col - 1):
                for way in (1, -1):
                    along(way, hops, lambda shard: left_copy(part, shard, way, hops).wait_send())
        if q < chunks - hybrid:
            for step in range(1, n_depth):
                for half in range(HALVES):
                    part_copy(q, step, half).wait_send()
    for layer in range(layers):
        for step in range(1, outers):
            right_copy(layer, step).wait_send()
        for step in range(outers):
            core_copy(layer, step).wait_send()
    if hybrid:
        for n in range(hybrid + 2):
            layer_copy(n).wait_send()


def per_device(sizes, left_blocks, right_blocks, triples):
    n_row, n_col, n_depth, order, groups, local_rows, share, chunks, hybrid = sizes
    width = groups * order
    pairs = share // 2
    layers = 2 if hybrid else 1
    f32, bf16, i32 = jnp.float32, jnp.bfloat16, jnp.int32
    dma = pltpu.SemaphoreType.DMA
    return pl.pallas_call(
        functools.partial(kernel, sizes),
        out_shape=jax.ShapeDtypeStruct((share, order, order), f32),
        in_specs=[pl.BlockSpec(memory_space=pl.ANY)] * 3,
        out_specs=pl.BlockSpec(memory_space=pltpu.VMEM),
        scratch_shapes=[
            pltpu.VMEM(left_blocks.shape, f32),
            pltpu.VMEM(right_blocks.shape, f32),
            pltpu.VMEM((layers,) + triples.shape, i32),
            pltpu.VMEM((chunks + hybrid, n_col, local_rows, CHUNK_ROWS, width), f32),
            pltpu.VMEM((layers, n_row, local_rows // 2, width, LANES), f32),
            pltpu.VMEM((layers, n_row * local_rows, width, LANES), bf16),
            pltpu.VMEM((chunks + hybrid, n_col * local_rows, 2 * CHUNK_ROWS, width), bf16),
            pltpu.VMEM((layers, PC, CHUNK_ROWS, width), bf16),
            pltpu.VMEM((layers, PC, width), f32),
            pltpu.VMEM((layers, PC, LANES), i32),
            pltpu.SMEM((layers, PC, LANES), i32),
            pltpu.VMEM((chunks, n_depth - 1, pairs, CHUNK_ROWS, LANES), f32),
            pltpu.VMEM((chunks, n_depth - 1, pairs, CHUNK_ROWS, LANES), f32),
            pltpu.VMEM((chunks, pairs, CHUNK_ROWS, LANES), f32),
            dma((chunks + hybrid, 2, n_col - 1)),
            dma((chunks + hybrid, 2, n_col - 1)),
            dma((layers, n_row // 2 - 1)),
            dma((layers, n_row // 2 - 1)),
            dma((layers, n_row // 2)),
            dma((layers, n_row // 2)),
            dma((chunks, n_depth - 1, HALVES)),
            dma((chunks, n_depth - 1, HALVES)),
            dma((layers,)),
            dma((3,)),
            dma((hybrid + 2,)),
            dma((hybrid + 2,)),
        ],
        compiler_params=pltpu.CompilerParams(
            collective_id=0, has_side_effects=True, vmem_limit_bytes=48 * 1024 * 1024
        ),
        cost_estimate=pl.CostEstimate(
            flops=2 * PC * 4 * order * width * order, bytes_accessed=8 * 1024 * 1024, transcendentals=0
        ),
        name="filtered_product",
    )(*(pltpu.with_memory_space_constraint(x, pltpu.HBM) for x in (left_blocks, right_blocks, triples)))


def solution(mesh):
    n_row, n_col, n_depth = mesh.shape["row"], mesh.shape["col"], mesh.shape["depth"]
    devices = n_row * n_col * n_depth
    placed = (
        P(("row", "col", "depth"), None, None),
        P(("row", "col", "depth"), None, None),
        P(None, ("row", "col", "depth")),
    )

    def whole(left_blocks, right_blocks, triples):
        local = left_blocks.shape[0] // devices
        order = left_blocks.shape[1]
        groups = max(1, local // 4)
        chunks = order // CHUNK_ROWS
        hybrid = HYBRID if n_depth == 2 and chunks >= HYBRID + 2 else 0
        sizes = (n_row, n_col, n_depth, order, groups, local // groups, PC // n_depth, chunks, hybrid)
        return jax.shard_map(
            functools.partial(per_device, sizes),
            mesh=mesh,
            in_specs=placed,
            out_specs=P(("row", "col", "depth"), None, None),
            check_vma=False,
        )(left_blocks, right_blocks, triples)

    return whole
```

time: 46.4 us -> 45.2 us (0.974)
  Pallas kernels: 44.9 us -> 43.7 us
    pallas_call x1, Pallas kernels: 44.9 us -> 43.7 us  [per_device(): pl.pallas_call(functools.partial(kernel, sizes), out_shape=jax.ShapeDtype...]
where the time goes in v5:
time: 45.2 us; the launch traced here: 45.1 us
  Pallas kernels  43.7 us (97%)
  local copies, waits for them, and re-layouts  1.32 us (3%)
    pallas_call x1, Pallas kernels, per_device(): pl.pallas_call(functools.partial(kernel, sizes), out_shape=jax.ShapeDtype...  43.7 us
    unnamed x1, local copies, waits for them, and re-layouts  1.32 us

profile of v5, /device:TPU:0, one launch (start us, length us, event | category | flops | bytes accessed | tf_op | source)
XLA Modules:
  0.0 45.1 jit_solution(15226140144571841312)
XLA Ops:
  0.0 43.7 %filtered_product.1 = f32[64,64,64]{2,1,0:T(8,128)S(1)} custom-call(f32[16,64,64]{2,1,0:T(8,128)} %left_hbm.1, f32[16,64,64]{2,1,0:T(8,128)} %right_hbm.1, s32[3,512]{1,0:T(4,128)} %triples_hbm.1), custom_call_target="tpu_custom_call" | custom-call | flops 1073741824 | bytes 8388608 | tf_op jit(solution)/shard_map/filtered_product/pallas_call | solution.py:395
  43.7 1.3 %copy.5 = f32[64,64,64]{2,1,0:T(8,128)} copy(f32[64,64,64]{2,1,0:T(8,128)S(1)} %filtered_product.1) | data formatting | bytes 2097152

commit v6 on v5

--- a/solution.py
+++ b/solution.py
@@ -1,4 +1,5 @@
 import functools
+import math
 
 import jax
 import jax.numpy as jnp
@@ -10,7 +11,7 @@
 PC = 128
 LANES = 128
 CHUNK_ROWS = 16
-UNROLL_PAIRS = 4
+UNROLL_PAIRS = 16
 HALVES = 2
 HYBRID = 1
 MESH = pl.DeviceIdType.MESH
@@ -244,6 +245,9 @@
         code_copy.wait()
 
     tabulate(0)
+    first_hops = list(range(1, n_col - 1))
+    for hops in first_hops[:1]:
+        left_arrive(0, hops)
     if hybrid:
         layer_copy(0).wait_recv()
         tabulate(1)
@@ -261,7 +265,7 @@
                 right_split[layer, at, rows, :] = jnp.where(lower, high, low).astype(jnp.bfloat16)
                 right_split[layer, at + 1, rows, :] = jnp.where(lower, low, high).astype(jnp.bfloat16)
 
-    for hops in range(1, n_col - 1):
+    for hops in first_hops[1:]:
         left_arrive(0, hops)
     split_right(0, row)
     core_copy(0, 0).wait_recv()
@@ -294,22 +298,25 @@
         used = mask_ref[layer, k]
         picked = picked * jnp.concatenate([used, used], axis=0)
         both = jnp.dot(picked, right_split[layer, codes[layer, k, 1]], preferred_element_type=jnp.float32)
-        both = both[:CHUNK_ROWS] + both[CHUNK_ROWS:]
-        return both + pltpu.roll(both, order, 1)
+        return both[:CHUNK_ROWS] + both[CHUNK_ROWS:]
+
+    unroll = math.gcd(UNROLL_PAIRS, pairs // HALVES)
 
     def products(parts, first, target, half):
         def body(turn_index, carry):
-            for inner in range(UNROLL_PAIRS):
-                p = turn_index * UNROLL_PAIRS + inner
+            for inner in range(unroll):
+                p = turn_index * unroll + inner
                 k = first + 2 * p
                 total = None
                 for layer, part in enumerate(parts):
-                    pair = jnp.where(lane_low, one_slot(layer, part, k), one_slot(layer, part, k + 1))
-                    total = pair if total is None else total + pair
-                target[p] = total
+                    even, odd = one_slot(layer, part, k), one_slot(layer, part, k + 1)
+                    straight = jnp.where(lane_low, even, odd)
+                    crossed = jnp.where(lane_low, odd, even)
+                    total = [straight, crossed] if total is None else [total[0] + straight, total[1] + crossed]
+                target[p] = total[0] + pltpu.roll(total[1], order, 1)
             return carry
 
-        turns = pairs // UNROLL_PAIRS // HALVES
+        turns = pairs // HALVES // unroll
         lax.fori_loop(half * turns, (half + 1) * turns, body, 0)
 
     def finish(q):

time: 45.2 us -> 38.7 us (0.86)
  Pallas kernels: 43.7 us -> 37.3 us
    pallas_call x1, Pallas kernels: 43.7 us -> 37.3 us  [per_device(): pl.pallas_call(functools.partial(kernel, sizes), out_shape=jax.ShapeDtype...]
where the time goes in v6:
time: 38.7 us; the launch traced here: 38.6 us
  Pallas kernels  37.3 us (96%)
  local copies, waits for them, and re-layouts  1.32 us (3%)
    pallas_call x1, Pallas kernels, per_device(): pl.pallas_call(functools.partial(kernel, sizes), out_shape=jax.ShapeDtype...  37.3 us
    unnamed x1, local copies, waits for them, and re-layouts  1.32 us

profile of v6, /device:TPU:0, one launch (start us, length us, event | category | flops | bytes accessed | tf_op | source)
XLA Modules:
  0.0 38.6 jit_solution(728660254510827794)
XLA Ops:
  0.0 37.3 %filtered_product.1 = f32[64,64,64]{2,1,0:T(8,128)S(1)} custom-call(f32[16,64,64]{2,1,0:T(8,128)} %left_hbm.1, f32[16,64,64]{2,1,0:T(8,128)} %right_hbm.1, s32[3,512]{1,0:T(4,128)} %triples_hbm.1), custom_call_target="tpu_custom_call" | custom-call | flops 1073741824 | bytes 8388608 | tf_op jit(solution)/shard_map/filtered_product/pallas_call | solution.py:402
  37.3 1.3 %copy.5 = f32[64,64,64]{2,1,0:T(8,128)} copy(f32[64,64,64]{2,1,0:T(8,128)S(1)} %filtered_product.1) | data formatting | bytes 2097152

commit v7 on v6

--- a/solution.py
+++ b/solution.py
@@ -100,13 +100,6 @@
         for g in range(groups):
             pair = jnp.concatenate([right_ref[j * groups + g], right_ref[(j + 1) * groups + g]], axis=-1)
             right_all[0, row, j // 2, g * order : (g + 1) * order, :] = pair
-    fetches[1].wait()
-    for i in range(local_rows):
-        for g in range(0, groups, 2):
-            pair = jnp.concatenate([left_ref[i * groups + g], left_ref[i * groups + g + 1]], axis=-1)
-            for q in range(chunks):
-                left_all[q, col, i, :, g * order : (g + 2) * order] = pair[q * CHUNK_ROWS : (q + 1) * CHUNK_ROWS]
-
     pl.semaphore_wait(barrier, greeted)
 
     def left_copy(q, shard, way, hops):
@@ -201,10 +194,16 @@
 
     for step in range(1, outers):
         right_copy(0, step).start()
+    core_copy(0, 0).start()
+    layers = 2 if hybrid else 1
+    fetches[1].wait()
+    for i in range(local_rows):
+        for g in range(0, groups, 2):
+            pair = jnp.concatenate([left_ref[i * groups + g], left_ref[i * groups + g + 1]], axis=-1)
+            for q in range(chunks):
+                left_all[q, col, i, :, g * order : (g + 2) * order] = pair[q * CHUNK_ROWS : (q + 1) * CHUNK_ROWS]
     left_start(0, 0)
-    core_copy(0, 0).start()
     fetches[2].wait()
-    layers = 2 if hybrid else 1
     if hybrid:
         for n in range(hybrid + 2):
             layer_copy(n).start()
@@ -347,15 +346,18 @@
                     high, low = split_bf16(left_all[part, shard, i])
                     left_split[part, shard * local_rows + i, :CHUNK_ROWS, :] = high
                     left_split[part, shard * local_rows + i, CHUNK_ROWS:, :] = low
+        hops_ahead = range(1, n_col - 1) if q + 1 < chunks else range(0)
+        for hops in hops_ahead[:1]:
+            for part in chunk_parts(q + 1):
+                left_arrive(part, hops)
         if q < chunks - hybrid:
             for step in range(1, n_depth):
                 partner = turn(depth, step, n_depth)
                 for half in range(HALVES):
                     products([q], partner * share, part_send.at[q, step - 1], half)
                     part_copy(q, step, half).start()
-        hops_ahead = range(1, n_col - 1) if q + 1 < chunks else range(0)
         for half in range(HALVES):
-            for hops in hops_ahead[half::HALVES]:
+            for hops in hops_ahead[1 + half :: HALVES]:
                 for part in chunk_parts(q + 1):
                     left_arrive(part, hops)
             products(chunk_parts(q), depth * share, part_own.at[q], half)
@@ -368,9 +370,9 @@
             split_right(1, other_core)
             for step in range(1, outers):
                 split_right(1, turn(outer + outers, -step, outers) * 2 + core)
-        if q > 0 and q < chunks - hybrid:
-            finish(q - 1)
-    for q in range(max(0, chunks - hybrid - 1), chunks):
+        if q > 1:
+            finish(q - 2)
+    for q in range(max(0, chunks - 2), chunks):
         finish(q)
 
     for q in range(chunks):

time: 38.7 us -> 38.8 us (level)
  no operation moved by 1% of the time
where the time goes in v7:
time: 38.8 us; the launch traced here: 38.7 us
  Pallas kernels  37.3 us (96%)
  local copies, waits for them, and re-layouts  1.32 us (3%)
    pallas_call x1, Pallas kernels, per_device(): pl.pallas_call(functools.partial(kernel, sizes), out_shape=jax.ShapeDtype...  37.3 us
    unnamed x1, local copies, waits for them, and re-layouts  1.32 us

profile of v7, /device:TPU:0, one launch (start us, length us, event | category | flops | bytes accessed | tf_op | source)
XLA Modules:
  0.0 38.7 jit_solution(4252065336255960555)
XLA Ops:
  0.0 37.3 %filtered_product.1 = f32[64,64,64]{2,1,0:T(8,128)S(1)} custom-call(f32[16,64,64]{2,1,0:T(8,128)} %left_hbm.1, f32[16,64,64]{2,1,0:T(8,128)} %right_hbm.1, s32[3,512]{1,0:T(4,128)} %triples_hbm.1), custom_call_target="tpu_custom_call" | custom-call | flops 1073741824 | bytes 8388608 | tf_op jit(solution)/shard_map/filtered_product/pallas_call | solution.py:404
  37.3 1.3 %copy.5 = f32[64,64,64]{2,1,0:T(8,128)} copy(f32[64,64,64]{2,1,0:T(8,128)S(1)} %filtered_product.1) | data formatting | bytes 2097152

commit v8 on v7

--- a/solution.py
+++ b/solution.py
@@ -301,7 +301,7 @@
 
     unroll = math.gcd(UNROLL_PAIRS, pairs // HALVES)
 
-    def products(parts, first, target, half):
+    def products(parts, first, target, half, unroll=unroll):
         def body(turn_index, carry):
             for inner in range(unroll):
                 p = turn_index * unroll + inner
@@ -315,7 +315,7 @@
                 target[p] = total[0] + pltpu.roll(total[1], order, 1)
             return carry
 
-        turns = pairs // HALVES // unroll
+        turns = max(1, pairs // HALVES // unroll)
         lax.fori_loop(half * turns, (half + 1) * turns, body, 0)
 
     def finish(q):
@@ -346,21 +346,21 @@
                     high, low = split_bf16(left_all[part, shard, i])
                     left_split[part, shard * local_rows + i, :CHUNK_ROWS, :] = high
                     left_split[part, shard * local_rows + i, CHUNK_ROWS:, :] = low
-        hops_ahead = range(1, n_col - 1) if q + 1 < chunks else range(0)
-        for hops in hops_ahead[:1]:
-            for part in chunk_parts(q + 1):
-                left_arrive(part, hops)
         if q < chunks - hybrid:
             for step in range(1, n_depth):
                 partner = turn(depth, step, n_depth)
                 for half in range(HALVES):
                     products([q], partner * share, part_send.at[q, step - 1], half)
                     part_copy(q, step, half).start()
-        for half in range(HALVES):
-            for hops in hops_ahead[1 + half :: HALVES]:
-                for part in chunk_parts(q + 1):
-                    left_arrive(part, hops)
-            products(chunk_parts(q), depth * share, part_own.at[q], half)
+        hops_ahead = range(1, n_col - 1) if q + 1 < chunks else range(0)
+        for hops in hops_ahead:
+            for part in chunk_parts(q + 1):
+                left_arrive(part, hops)
+        if q < chunks - hybrid:
+            products([q], depth * share, part_own.at[q], 0, pairs)
+        else:
+            for half in range(HALVES):
+                products(chunk_parts(q), depth * share, part_own.at[q], half)
         if hybrid and q == 0:
             right_pass(1, False)
         if hybrid and q == 1:
@@ -370,9 +370,9 @@
             split_right(1, other_core)
             for step in range(1, outers):
                 split_right(1, turn(outer + outers, -step, outers) * 2 + core)
-        if q > 1:
-            finish(q - 2)
-    for q in range(max(0, chunks - 2), chunks):
+        if q > 0 and q < chunks - hybrid:
+            finish(q - 1)
+    for q in range(max(0, chunks - hybrid - 1), chunks):
         finish(q)
 
     for q in range(chunks):

time: 38.8 us -> 39.4 us (1.015)
  Pallas kernels: 37.3 us -> 37.9 us
    pallas_call x1, Pallas kernels: 37.3 us -> 37.9 us  [per_device(): pl.pallas_call(functools.partial(kernel, sizes), out_shape=jax.ShapeDtype...]
where the time goes in v8:
time: 39.4 us; the launch traced here: 39.2 us
  Pallas kernels  37.9 us (96%)
  local copies, waits for them, and re-layouts  1.32 us (3%)
    pallas_call x1, Pallas kernels, per_device(): pl.pallas_call(functools.partial(kernel, sizes), out_shape=jax.ShapeDtype...  37.9 us
    unnamed x1, local copies, waits for them, and re-layouts  1.32 us

profile of v8, /device:TPU:0, one launch (start us, length us, event | category | flops | bytes accessed | tf_op | source)
XLA Modules:
  0.0 39.2 jit_solution(4334682431968305075)
XLA Ops:
  0.0 37.9 %filtered_product.1 = f32[64,64,64]{2,1,0:T(8,128)S(1)} custom-call(f32[16,64,64]{2,1,0:T(8,128)} %left_hbm.1, f32[16,64,64]{2,1,0:T(8,128)} %right_hbm.1, s32[3,512]{1,0:T(4,128)} %triples_hbm.1), custom_call_target="tpu_custom_call" | custom-call | flops 1073741824 | bytes 8388608 | tf_op jit(solution)/shard_map/filtered_product/pallas_call | solution.py:404
  37.9 1.3 %copy.5 = f32[64,64,64]{2,1,0:T(8,128)} copy(f32[64,64,64]{2,1,0:T(8,128)S(1)} %filtered_product.1) | data formatting | bytes 2097152
